TPU v7x, 512 devices: a whole 4x4x16 slice. The times are simulated.
512 devices in a mesh: ctx: 64 (over y, z_hi, x, core), tp: 8 (over z_lo).
Axes of the slice: x: 4, y: 4, z: 16 (z_hi: 2, z_lo: 8; z = z_hi * 8 + z_lo), core: 2. Of those that a mesh axis runs over, the one named last changes fastest.
Arguments:
- q_self: bfloat16 [8192, 3072], P('ctx', 'tp'), may hold values from -200 to 200
- k_self: bfloat16 [8192, 3072], P('ctx', 'tp'), may hold values from -6 to 6
- v_self: bfloat16 [8192, 3072], P('ctx', 'tp'), may hold values from -12 to 12
- q_cross: bfloat16 [8192, 3072], P('ctx', 'tp'), may hold values from -200 to 200
- k_text: bfloat16 [256, 3072], P('ctx', 'tp'), may hold values from -6 to 6
- v_text: bfloat16 [256, 3072], P('ctx', 'tp'), may hold values from -12 to 12
- text_len: int32 [1], replicated, may hold values from 64 to 256
- timestep: int32 [1], replicated, may hold values from 0 to 999
- gate_table: float32 [1000, 3072], P(None, 'tp'), may hold values from -4 to 4
Outputs:
- attended: bfloat16 [8192, 3072], P(('ctx', 'tp'))
Inputs may be any that keep to these rules, and one draw needn't show every extreme that they name: Text positions from text_len on are padding.
All inputs are finite; a program needn't handle non-finite values.
Results may differ from a plain program's by a relative error of at most 0.0033.
Values may be sent and summed in bfloat16 or wider, within the bound.
A program may use at most 64 MiB of HBM per device.

v0:
```python
import math

import jax
import jax.numpy as jnp
from jax import lax
from jax.sharding import PartitionSpec as P

HD = 128


def empty_state(head_count, local_rows):
    return (
        jnp.full((head_count, local_rows), -jnp.inf, jnp.float32),
        jnp.zeros((head_count, local_rows), jnp.float32),
        jnp.zeros((head_count, local_rows, HD), jnp.float32),
    )


def absorb(carry_state, queries, keys, values, key_bias):
    key_count = keys.shape[0]
    head_count = queries.shape[1]
    block_rows = math.gcd(key_count, 1024)
    block_count = key_count // block_rows

    def absorb_block(running, pieces):
        key_block, value_block, bias_block = pieces
        key_heads = key_block.reshape(block_rows, head_count, HD)
        value_heads = value_block.reshape(block_rows, head_count, HD)
        scores = jnp.einsum(
            "lhd,shd->hls", queries, key_heads, preferred_element_type=jnp.float32
        ) * HD ** (-0.5)
        scores = scores + bias_block[None, None, :]
        row_max, row_sum, accum = running
        new_max = jnp.maximum(row_max, jnp.max(scores, axis=2))
        factor = jnp.exp(row_max - new_max)
        weights = jnp.exp(scores - new_max[:, :, None])
        row_sum = row_sum * factor + jnp.sum(weights, axis=2)
        accum = accum * factor[:, :, None] + jnp.einsum(
            "hls,shd->hld",
            weights.astype(jnp.bfloat16),
            value_heads,
            preferred_element_type=jnp.float32,
        )
        return ((new_max, row_sum, accum), None)

    pieces = (
        keys.reshape(block_count, block_rows, keys.shape[1]),
        values.reshape(block_count, block_rows, values.shape[1]),
        key_bias.reshape(block_count, block_rows),
    )
    carry_state, unused = lax.scan(absorb_block, carry_state, pieces)
    return carry_state


def finish(carry_state):
    accum = carry_state[2] / carry_state[1][:, :, None]
    return accum.transpose(1, 0, 2).reshape(accum.shape[1], accum.shape[0] * HD)


def local(q_self, k_self, v_self, q_cross, k_text, v_text, text_len, timestep, gate_table):
    local_rows = q_self.shape[0]
    head_count = q_self.shape[1] // HD
    gate_row = lax.dynamic_index_in_dim(gate_table, timestep[0], 0, keepdims=False)
    self_queries = q_self.reshape(local_rows, head_count, HD)
    cross_queries = q_cross.reshape(local_rows, head_count, HD)
    start_state = empty_state(head_count, local_rows)
    all_keys = lax.all_gather(k_self, "ctx", axis=0, tiled=True)
    all_values = lax.all_gather(v_self, "ctx", axis=0, tiled=True)
    zero_bias = jnp.zeros((all_keys.shape[0],), jnp.float32)
    final_state = absorb(start_state, self_queries, all_keys, all_values, zero_bias)
    self_out = finish(final_state)
    text_keys = lax.all_gather(k_text, "ctx", axis=0, tiled=True)
    text_values = lax.all_gather(v_text, "ctx", axis=0, tiled=True)
    positions = jnp.arange(text_keys.shape[0], dtype=jnp.int32)
    key_bias = jnp.where(positions < text_len[0], 0.0, -jnp.inf).astype(jnp.float32)
    start_state = empty_state(head_count, local_rows)
    cross_out = finish(absorb(start_state, cross_queries, text_keys, text_values, key_bias))
    attended = (gate_row[None, :] * self_out + cross_out).astype(jnp.bfloat16)
    return lax.all_to_all(attended, "tp", split_axis=0, concat_axis=1, tiled=True)


def solution(mesh):
    placed = (
        P("ctx", "tp"),
        P("ctx", "tp"),
        P("ctx", "tp"),
        P("ctx", "tp"),
        P("ctx", "tp"),
        P("ctx", "tp"),
        P(),
        P(),
        P(None, "tp"),
    )
    return jax.shard_map(
        local, mesh=mesh, in_specs=placed, out_specs=P(("ctx", "tp"), None), check_vma=False
    )
```

profile of v0, /device:TPU:1, one launch (start us, length us, event | category | flops | bytes accessed | tf_op | source)
XLA Modules:
  0.0 430.3 jit_solution(5190741893535849852)
XLA Ops:
  9.3 1.0 copy.40
  10.5 1.0 copy.45
  11.5 181.3 %all-gather = bf16[64,4,384]{2,1,0:T(4,128)(2,1)S(1)} all-gather(bf16[1,4,384]{2,1,0:T(4,128)(2,1)} %bitcast.68), channel_id=1, replica_groups=mesh['ctx'=64,'tp'=8] {'ctx'}, dimensions={0}, use_global_device_ids=true | all-gather | bytes 199680 | tf_op jit(solution)/shard_map/all_gather | solution.py:72
  192.9 156.6 %all-gather.1 = bf16[64,4,384]{2,1,0:T(4,128)(2,1)S(1)} all-gather(bf16[1,4,384]{2,1,0:T(4,128)(2,1)} %bitcast.69), channel_id=1, replica_groups=mesh['ctx'=64,'tp'=8] {'ctx'}, dimensions={0}, use_global_device_ids=true | all-gather | bytes 199680 | tf_op jit(solution)/shard_map/all_gather | solution.py:73
  350.6 0.8 reshape.79
  351.5 43.5 %while.3 = (s32[]{:T(128)}, f32[3,128]{1,0:T(4,128)S(1)}, f32[3,128]{1,0:T(4,128)S(1)}, f32[3,128,128]{2,1,0:T(8,128)S(1)}, bf16[8,1024,384]{2,1,0:T(8,128)(2,1)...) while((s32[]{:T(128)}, f32[3,128]{1,0:T(4,128)S(1)}, ...), condition=%wide.region_3.4_spmd.clone, body=%wide.region_0.3_spmd.clone.sunk | while | flops 203835264 | bytes 13099125 | solution.py:51
  351.5 2.5 constant_dynamic-slice_fusion.3
  354.3 1.4 copy.67
  357.0 2.5 constant_dynamic-slice_fusion.3
  359.7 1.4 copy.67
  362.4 2.5 constant_dynamic-slice_fusion.3
  365.2 1.4 copy.67
  367.8 2.5 constant_dynamic-slice_fusion.3
  370.6 1.4 copy.67
  373.3 2.5 constant_dynamic-slice_fusion.3
  376.0 1.4 copy.67
  378.7 2.5 constant_dynamic-slice_fusion.3
  381.5 1.4 copy.67
  384.1 2.5 constant_dynamic-slice_fusion.3
  386.9 1.4 copy.67
  389.6 2.5 constant_dynamic-slice_fusion.3
  392.3 1.4 copy.67
  395.4 1.0 add_convert_fusion
  396.4 26.5 %all_to_all.16 = bf16[8,16,384]{2,1,0:T(8,128)(2,1)S(1)} all-to-all(bf16[8,16,384]{2,1,0:T(8,128)(2,1)S(1)} %add_convert_fusion), channel_id=1, replica_groups=mesh['ctx'=64,'tp'=8] {'tp'}, dimensions={0} | all-to-all | bytes 196608 | tf_op jit(solution)/shard_map/all_to_all | solution.py:79
  (82 shorter events, 16.0 us)
Async XLA Ops:
  6.5 344.9 %copy-start = (f32[1000,384]{1,0:T(8,128)S(1)}, f32[1000,384]{1,0:T(8,128)}, u32[]{:S(2)}) copy-start(f32[1000,384]{1,0:T(8,128)} %param.19) | copy-start | bytes 4608004
  6.5 344.9 %all-gather.5.cloned.1.call-start = ((), (), s32[]{:S(2)}) async-start(), calls=%async_computation.1 | async-start | bytes 6389760 | tf_op jit(solution)/shard_map/all_gather | solution.py:67
  7.3 344.2 %all-gather.7.cloned.1.call-start = ((), (), s32[]{:S(2)}) async-start(), calls=%async_computation.2 | async-start | bytes 6389760 | tf_op jit(solution)/shard_map/all_gather | solution.py:68
Sparse Core Ops, SparseCore 0:
  11.9 159.5 all-gather.4
  176.0 143.4 all-gather.6
where the time goes:
time: 433 us; the launch traced here: 430 us
  blocking collectives  364 us (84%)
  local copies, waits for them, and re-layouts  37.4 us (9%)
  between operations  14.8 us (3%)
  matrix products  8.42 us (2%)
    all_gather x1, blocking collectives, local(): text_keys = lax.all_gather(k_text, 'ctx', axis=0, tiled=True)  181 us
    all_gather x1, blocking collectives, local(): text_values = lax.all_gather(v_text, 'ctx', axis=0, tiled=True)  157 us
    dynamic_slice x24, local copies, waits for them, and re-layouts, absorb(): carry_state, unused = lax.scan(absorb_block, carry_state, pieces)  33.3 us
    all_to_all x1, blocking collectives, local(): lax.all_to_all(attended, 'tp', split_axis=0, concat_axis=1, tiled=True)  26.5 us
  transfers between devices with their start and end apart: 2, of which 0 were waited for; matrix products, arithmetic and copies ran while one was open for 1% of the time, Pallas kernels for 0%

commit v1 on v0

v1 whole, which is shorter than its diff:
```python
import jax
import jax.numpy as jnp
from jax import lax
from jax.experimental import pallas as pl
from jax.experimental.pallas import tpu as pltpu
from jax.sharding import PartitionSpec as P

HD = 128
ROWS = 128
NH = 3
NX = 4
NY = 4
NT = 8
CHUNK = ROWS // NT
KEYS = NX * NY * ROWS
SCALE2 = HD ** -0.5 * 1.4426950408889634
MESH_ID = pl.DeviceIdType.MESH
SENDS = 192
RECVS = 96


def kernel(
    text_len, timestep, q_ref, k_ref, v_ref, qc_ref, kt_ref, vt_ref, gate_ref, out_ref,
    kb, vb, qb, qcb, gate, txb, tk, acc, sts, racc, rsts, xs, so, xr, sr, cs, cr, wt, ktv, vtv, grow,
    ssem, rsem, lsem,
):
    ctx = lax.axis_index("ctx")
    zl = lax.axis_index("tp")
    y = ctx // 16
    zh = (ctx // 8) % 2
    x = (ctx // 2) % 4
    c = ctx % 2

    def dev(dy=0, dx=0, flip_z=False, flip_c=False, dz=0):
        yy = (y + dy) % NY
        xx = (x + dx) % NX
        zz = 1 - zh if flip_z else zh
        cc = 1 - c if flip_c else c
        return (((yy * 2 + zz) * 4 + xx) * 2 + cc, (zl + dz) % NT)

    sent = []
    counts = {"s": 0, "r": 0, "l": 0}

    def new(kind, n=1):
        first = counts[kind]
        counts[kind] = first + n
        return first

    def send(src, dst, rs, target):
        cp = pltpu.make_async_remote_copy(
            src_ref=src, dst_ref=dst, send_sem=ssem.at[new("s")], recv_sem=rsem.at[rs],
            device_id=target, device_id_type=MESH_ID,
        )
        cp.start()
        sent.append(cp)

    def arrived(ref, rs):
        pltpu.make_async_copy(ref, ref, rsem.at[rs]).wait()

    def fetch(src, dst):
        cp = pltpu.make_async_copy(src, dst, lsem.at[new("l")])
        cp.start()
        return cp

    def cols(h):
        return pl.ds(h * HD, HD)

    barrier = pltpu.get_barrier_semaphore()
    partners = [dev(dx=d) for d in (1, 2, 3)] + [dev(dy=d) for d in (1, 2, 3)]
    partners += [dev(flip_c=True)]
    partners += [dev(dz=d) for d in range(1, NT)] + [dev(dz=d, flip_z=True) for d in range(NT)]
    for partner in partners:
        pl.semaphore_signal(barrier, inc=1, device_id=partner, device_id_type=MESH_ID)

    local = []
    for h in range(NH):
        local.append(fetch(k_ref.at[:, cols(h)], kb.at[h, y, x]))
        local.append(fetch(v_ref.at[:, cols(h)], vb.at[h, y, x]))
        local.append(fetch(q_ref.at[:, cols(h)], qb.at[0, 0, h]))
    late = [fetch(qc_ref, qcb), fetch(gate_ref, gate)]
    zc = zh * 2 + c
    zo = (1 - zh) * 2 + c
    for cp in (fetch(kt_ref, ktv), fetch(vt_ref, vtv)):
        cp.wait()
    txb[zc] = jnp.concatenate(
        [ktv[...].astype(jnp.float32), vtv[...].astype(jnp.float32)], axis=0
    )
    pl.semaphore_wait(barrier, len(partners))

    sib = dev(flip_c=True)
    across = dev(flip_z=True)

    r_k1 = [[new("r") for d in range(3)] for h in range(NH)]
    r_v1 = [[new("r") for d in range(3)] for h in range(NH)]
    r_k2 = [[new("r") for d in range(2)] for h in range(NH)]
    r_v2 = [[new("r") for d in range(2)] for h in range(NH)]
    r_k3 = [[new("r") for d in range(2)] for h in range(NH)]
    r_v3 = [[new("r") for d in range(2)] for h in range(NH)]
    r_q01 = [new("r") for h in range(NH)]
    r_q10 = [new("r") for h in range(NH)]
    r_q11 = [new("r") for h in range(NH)]
    r_tz, r_ts, r_tzs = new("r"), new("r"), new("r")
    r_t1 = [new("r") for d in range(3)]
    r_t2 = [new("r") for d in range(3)]
    r_t3 = new("r")
    r_acc = [[new("r") for h in range(NH)] for p in range(2)]
    r_sts = [[new("r") for h in range(NH)] for p in range(2)]
    r_x = [[new("r") for h in range(NH)] for p in range(2)]
    r_s = [[new("r") for h in range(NH)] for p in range(2)]
    r_c = new("r")

    def first(h):
        for d in (1, 3, 2):
            send(k_ref.at[:, cols(h)], kb.at[h, y, x], r_k1[h][d - 1], dev(dx=d))
            send(v_ref.at[:, cols(h)], vb.at[h, y, x], r_v1[h][d - 1], dev(dy=d))

    def second(h):
        for d in (1, 2, 3):
            arrived(kb.at[h, y, (x - d + NX) % NX], r_k1[h][d - 1])
            arrived(vb.at[h, (y - d + NY) % NY, x], r_v1[h][d - 1])
        for i, d in ((0, 1), (1, 3)):
            send(kb.at[h, y], kb.at[h, y], r_k2[h][i], dev(dy=d))
            send(vb.at[h, :, x], vb.at[h, :, x], r_v2[h][i], dev(dx=d))

    def relay(h):
        for i, d in ((0, 1), (1, 3)):
            yo = (y - d + NY) % NY
            xo = (x - d + NX) % NX
            half = pl.ds(2 * i, 2)
            arrived(kb.at[h, yo], r_k2[h][i])
            send(kb.at[h, yo, half], kb.at[h, yo, half], r_k3[h][i], dev(dy=d))
            arrived(vb.at[h, :, xo], r_v2[h][i])
            send(vb.at[h, half, xo], vb.at[h, half, xo], r_v3[h][i], dev(dx=d))

    def complete(h):
        yo = (y + 2) % NY
        xo = (x + 2) % NX
        for i in range(2):
            half = pl.ds(2 * i, 2)
            arrived(kb.at[h, yo, half], r_k3[h][i])
            arrived(vb.at[h, half, xo], r_v3[h][i])

    def attend(h, p):
        keys = lambda: kb[h].reshape(KEYS, HD)
        values = lambda: vb[h].reshape(KEYS, HD)

        def body(i, unused):
            o = 1 - i
            scores = lax.dot_general(
                qb[p, o, h], keys(), (((1,), (1,)), ((), ())), preferred_element_type=jnp.float32
            )
            top = jnp.max(scores, axis=1, keepdims=True)
            weights = jnp.exp2((scores - top) * SCALE2)
            total = jnp.sum(weights, axis=1, keepdims=True)
            acc[p, h, o] = jnp.dot(
                weights.astype(jnp.bfloat16), values(), preferred_element_type=jnp.float32
            )
            lane = lax.broadcasted_iota(jnp.int32, (ROWS, HD), 1)
            sts[p, h, o] = jnp.where(lane < HD // 2, top, total)
            return unused

        lax.fori_loop(0, 2, body, 0)
        send(acc.at[p, h, 1], racc.at[p, h], r_acc[p][h], sib)
        send(sts.at[p, h, 1], rsts.at[p, h], r_sts[p][h], sib)

    def merge(h, p):
        arrived(racc.at[p, h], r_acc[p][h])
        arrived(rsts.at[p, h], r_sts[p][h])
        one, two = sts[p, h, 0], rsts[p, h]
        top1, sum1 = one[:, :1], one[:, HD // 2 : HD // 2 + 1]
        top2, sum2 = two[:, :1], two[:, HD // 2 : HD // 2 + 1]
        top = jnp.maximum(top1, top2)
        f1 = jnp.exp2((top1 - top) * SCALE2)
        f2 = jnp.exp2((top2 - top) * SCALE2)
        total = sum1 * f1 + sum2 * f2
        g = grow[:, h * HD : (h + 1) * HD]
        mixed = (acc[p, h, 0] * f1 + racc[p, h] * f2) / total * g
        xs[p, h] = mixed.astype(jnp.bfloat16).reshape(NT, CHUNK, HD)
        lane = lax.broadcasted_iota(jnp.int32, (ROWS, HD), 1)
        flat = jnp.where(lane < HD // 2, top, total).T
        so[p, h] = jnp.concatenate([flat[:1], flat[HD // 2 : HD // 2 + 1]], axis=0)
        for d in range(NT) if p == 1 else range(1, NT):
            target = dev(dz=d, flip_z=p == 1)
            send(xs.at[p, h, (zl + d) % NT], xr.at[p, h, zl], r_x[p][h], target)
            send(so.at[p, h], sr.at[p, h, zl], r_s[p][h], target)
        if p == 0:
            pltpu.make_async_copy(xs.at[p, h, zl], xr.at[p, h, zl], rsem.at[r_x[p][h]]).start()
            pltpu.make_async_copy(so.at[p, h], sr.at[p, h, zl], rsem.at[r_s[p][h]]).start()

    first(0)
    send(txb.at[zc], txb.at[zc], r_tz, across)
    send(txb.at[zc], txb.at[zc], r_ts, sib)
    for h in range(NH):
        send(q_ref.at[:, cols(h)], qb.at[1, 0, h], r_q10[h], across)
        send(q_ref.at[:, cols(h)], qb.at[0, 1, h], r_q01[h], sib)
    first(1)
    for cp in local:
        cp.wait()
    second(0)
    first(2)
    second(1)

    arrived(txb.at[zo], r_tz)
    send(txb.at[zo], txb.at[zo], r_tzs, sib)
    arrived(txb.at[zh * 2 + 1 - c], r_ts)
    arrived(txb.at[(1 - zh) * 2 + 1 - c], r_tzs)
    tiles = [txb[i] for i in range(4)]
    own = jnp.concatenate([jnp.where(c == 0, t[:4], t[4:]) for t in tiles], axis=0)
    tk[c, y, x] = own.astype(jnp.bfloat16)
    for d in (1, 2, 3):
        send(tk.at[c, y, x], tk.at[c, y, x], r_t1[d - 1], dev(dx=d))
    relay(0)
    second(2)
    for d in (1, 2, 3):
        arrived(tk.at[c, y, (x - d + NX) % NX], r_t1[d - 1])
    for d in (1, 2, 3):
        send(tk.at[c, y], tk.at[c, y], r_t2[d - 1], dev(dy=d))
    relay(1)
    for h in range(NH):
        arrived(qb.at[0, 1, h], r_q01[h])
    complete(0)
    attend(0, 0)
    arrived(qb.at[1, 0, 0], r_q10[0])
    send(qb.at[1, 0, 0], qb.at[1, 1, 0], r_q11[0], sib)
    for d in (1, 2, 3):
        arrived(tk.at[c, (y - d + NY) % NY], r_t2[d - 1])
    send(tk.at[c], tk.at[c], r_t3, sib)
    relay(2)
    complete(1)
    attend(1, 0)
    for cp in late:
        cp.wait()
    here = lax.broadcasted_iota(jnp.int32, gate.shape, 0) == timestep[0]
    grow[...] = jnp.sum(jnp.where(here, gate[...], 0.0), axis=0, keepdims=True)
    merge(0, 0)
    arrived(qb.at[1, 1, 0], r_q11[0])
    attend(0, 1)
    merge(1, 0)
    for h in (1, 2):
        arrived(qb.at[1, 0, h], r_q10[h])
        send(qb.at[1, 0, h], qb.at[1, 1, h], r_q11[h], sib)
    merge(0, 1)

    arrived(tk.at[1 - c], r_t3)
    j = lax.broadcasted_iota(jnp.int32, (ROWS, NX * NY * 16), 1)
    jy, jx, jz, jc, jr = j >> 6, (j >> 4) & 3, (j >> 3) & 1, (j >> 2) & 1, j & 3
    position = ((((jy * 2 + jz) * 4 + jx) * 2 + jc) << 2) + jr
    live = position < text_len[0]
    for h in range(NH):
        lanes = slice(h * HD, (h + 1) * HD)
        text_keys = tk[0].reshape(NX * NY * 16, NH * HD)[:, lanes]
        text_values = tk[1].reshape(NX * NY * 16, NH * HD)[:, lanes]
        scores = lax.dot_general(
            qcb[:, lanes], text_keys, (((1,), (1,)), ((), ())), preferred_element_type=jnp.float32
        )
        scores = jnp.where(live, scores, -jnp.inf)
        top = jnp.max(scores, axis=1, keepdims=True)
        weights = jnp.exp2((scores - top) * SCALE2)
        total = jnp.sum(weights, axis=1, keepdims=True)
        product = jnp.dot(
            weights.astype(jnp.bfloat16), text_values, preferred_element_type=jnp.float32
        )
        cs[:, :, lanes] = (product / total).astype(jnp.bfloat16).reshape(NT, CHUNK, HD)
    for d in range(1, NT):
        send(cs.at[(zl + d) % NT], cr.at[zl], r_c, dev(dz=d))
    pltpu.make_async_copy(cs.at[zl], cr.at[zl], rsem.at[r_c]).start()

    arrived(qb.at[1, 1, 1], r_q11[1])
    arrived(qb.at[1, 1, 2], r_q11[2])
    attend(1, 1)
    complete(2)
    attend(2, 1)
    merge(1, 1)
    attend(2, 0)
    merge(2, 1)
    merge(2, 0)

    arrived(cr, r_c)
    for p in range(2):
        for h in range(NH):
            arrived(xr.at[p, h], r_x[p][h])
            arrived(sr.at[p, h], r_s[p][h])
    shares = [[], []]
    for h in range(NH):
        one, two = sr[0, h], sr[1, h]
        top1, sum1, top2, sum2 = one[:, 0], one[:, 1], two[:, 0], two[:, 1]
        top = jnp.maximum(top1, top2)
        part1 = sum1 * jnp.exp2((top1 - top) * SCALE2)
        part2 = sum2 * jnp.exp2((top2 - top) * SCALE2)
        whole = part1 + part2
        shares[0].append(part1 / whole)
        shares[1].append(part2 / whole)
    rows = shares[0] + shares[1]
    table = jnp.concatenate(rows + [jnp.zeros((HD - NT * len(rows), HD), jnp.float32)], axis=0)
    wt[...] = table.T
    mine = wt[pl.ds(pl.multiple_of(zl * CHUNK, CHUNK), CHUNK), :]
    for src in range(NT):
        for h in range(NH):
            i, k = h * NT + src, (NH + h) * NT + src
            joined = xr[0, h, src].astype(jnp.float32) * mine[:, i : i + 1]
            joined = joined + xr[1, h, src].astype(jnp.float32) * mine[:, k : k + 1]
            joined = joined + cr[src, :, h * HD : (h + 1) * HD].astype(jnp.float32)
            lo = (src * NH + h) * HD
            out_ref[:, lo : lo + HD] = joined.astype(jnp.bfloat16)

    for cp in sent:
        cp.wait_send()
    assert counts["s"] <= SENDS and counts["r"] <= RECVS, counts


def local(q_self, k_self, v_self, q_cross, k_text, v_text, text_len, timestep, gate_table):
    bf16, f32 = jnp.bfloat16, jnp.float32
    smem = pl.BlockSpec(memory_space=pltpu.SMEM)
    vmem = pl.BlockSpec(memory_space=pltpu.VMEM)
    hbm = pl.BlockSpec(memory_space=pltpu.HBM)
    return pl.pallas_call(
        kernel,
        out_shape=jax.ShapeDtypeStruct((CHUNK, NT * NH * HD), bf16),
        in_specs=[smem, smem, hbm, hbm, hbm, hbm, hbm, hbm, hbm],
        out_specs=vmem,
        scratch_shapes=[
            pltpu.VMEM((NH, NY, NX, ROWS, HD), bf16),
            pltpu.VMEM((NH, NY, NX, ROWS, HD), bf16),
            pltpu.VMEM((2, 2, NH, ROWS, HD), bf16),
            pltpu.VMEM((ROWS, NH * HD), bf16),
            pltpu.VMEM(gate_table.shape, f32),
            pltpu.VMEM((4, 8, NH * HD), f32),
            pltpu.VMEM((2, NY, NX, 16, NH * HD), bf16),
            pltpu.VMEM((2, NH, 2, ROWS, HD), f32),
            pltpu.VMEM((2, NH, 2, ROWS, HD), f32),
            pltpu.VMEM((2, NH, ROWS, HD), f32),
            pltpu.VMEM((2, NH, ROWS, HD), f32),
            pltpu.VMEM((2, NH, NT, CHUNK, HD), bf16),
            pltpu.VMEM((2, NH, 2, HD), f32),
            pltpu.VMEM((2, NH, NT, CHUNK, HD), bf16),
            pltpu.VMEM((2, NH, NT, 2, HD), f32),
            pltpu.VMEM((NT, CHUNK, NH * HD), bf16),
            pltpu.VMEM((NT, CHUNK, NH * HD), bf16),
            pltpu.VMEM((HD, HD), f32),
            pltpu.VMEM(k_text.shape, bf16),
            pltpu.VMEM(v_text.shape, bf16),
            pltpu.VMEM((1, NH * HD), f32),
            pltpu.SemaphoreType.DMA((SENDS,)),
            pltpu.SemaphoreType.DMA((RECVS,)),
            pltpu.SemaphoreType.DMA((16,)),
        ],
        compiler_params=pltpu.CompilerParams(
            collective_id=0, has_side_effects=True, vmem_limit_bytes=64 * 1024 * 1024
        ),
        name="gated_attention",
    )(text_len, timestep, q_self, k_self, v_self, q_cross, k_text, v_text, gate_table)


def solution(mesh):
    placed = (
        P("ctx", "tp"),
        P("ctx", "tp"),
        P("ctx", "tp"),
        P("ctx", "tp"),
        P("ctx", "tp"),
        P("ctx", "tp"),
        P(),
        P(),
        P(None, "tp"),
    )
    return jax.shard_map(
        local, mesh=mesh, in_specs=placed, out_specs=P(("ctx", "tp"), None), check_vma=False
    )
```

time: 433 us -> 65.6 us (0.15)
  blocking collectives: 364 us -> 0 us
  Pallas kernels: 0 us -> 62.6 us
  local copies, waits for them, and re-layouts: 37.4 us -> 1.54 us
  between operations: 14.8 us -> 1.3 us
  matrix products: 8.42 us -> 0 us
    all_gather x2 -> x0, blocking collectives: 338 us -> none  [the longest x1 181 us: local(): text_keys = lax.all_gather(k_text, 'ctx', axis=0, tiled=True)]
    pallas_call x0 -> x1, Pallas kernels: none -> 62.6 us  [local(): pl.pallas_call(kernel, out_shape=jax.ShapeDtypeStruct((CHUNK, NT * NH * H...]
    dynamic_slice x25 -> x0, local copies, waits for them, and re-layouts: 33.3 us -> none  [the longest x24 33.3 us: absorb(): carry_state, unused = lax.scan(absorb_block, carry_state, pieces)]
    all_to_all x1 -> x0, blocking collectives: 26.5 us -> none  [local(): lax.all_to_all(attended, 'tp', split_axis=0, concat_axis=1, tiled=True)]
    dot_general x18 -> x0, matrix products: 8.42 us -> none  [the longest x9 4.43 us: absorb_block(): jnp.einsum('hls,shd->hld', weights.astype(jnp.bfloat16), value_heads, pre...]
  transfers between devices with their start and end apart: 2 -> 0, of which waited for: 0 -> 0; matrix products, arithmetic and copies ran while one was open for 1% -> 0% of each run, Pallas kernels for 0% -> 0%
where the time goes in v1:
time: 65.6 us; the launch traced here: 65.4 us
  Pallas kernels  62.6 us (95%)
  local copies, waits for them, and re-layouts  1.54 us (2%)
  between operations  1.3 us (2%)
    pallas_call x1, Pallas kernels, local(): pl.pallas_call(kernel, out_shape=jax.ShapeDtypeStruct((CHUNK, NT * NH * H...  62.6 us
    unnamed x1, local copies, waits for them, and re-layouts  1.54 us

profile of v1, /device:TPU:1, one launch (start us, length us, event | category | flops | bytes accessed | tf_op | source)
XLA Modules:
  0.0 65.4 jit_solution(4149203345372006079)
XLA Ops:
  1.3 62.6 %gated_attention.1 = bf16[16,3072]{1,0:T(8,128)(2,1)} custom-call(s32[1]{0:T(128)S(6)} %copy.11.text_len, s32[1]{0:T(128)S(6)} %copy.12.timestep, bf16[128,384]{1,0:T(8,128)(2,1)} %q_ref.1, bf16[128,384]{1,0:T(8,128)(2,1)} %k_ref.1, bf16[128,384]{1,0:T(8,128)(2,1)} %v_ref.1, bf16[128,384]{1,0:T(8,128)(2,1)} %qc_ref.1, bf16[4,384]{1,0:T(4,128)(2,1)} %kt_ref.1, ...), custom_call_target="tpu_custom_call" | custom-call | tf_op jit(solution)/shard_map/gated_attention/pallas_call | solution.py:316
  63.9 1.5 %copy.13 = bf16[16,3072]{1,0:T(8,128)(2,1)} copy(bf16[16,3072]{1,0:T(8,128)(2,1)} %gated_attention.1) | data formatting | bytes 196608

commit v2 on v1

v2 whole, which is shorter than its diff:
```python
import jax
import jax.numpy as jnp
from jax import lax
from jax.experimental import pallas as pl
from jax.experimental.pallas import tpu as pltpu
from jax.sharding import PartitionSpec as P

HD = 128
ROWS = 128
NH = 3
NX = 4
NY = 4
NT = 8
CHUNK = ROWS // NT
KEYS = NX * NY * ROWS
TEXT = NX * NY * 16
SCALE2 = HD ** -0.5 * 1.4426950408889634
MESH_ID = pl.DeviceIdType.MESH
SENDS = 192
RECVS = 96


def kernel(
    text_len, timestep, q_ref, k_ref, v_ref, qc_ref, kt_ref, vt_ref, gate_ref, out_ref,
    kb, vb, qb, qf, qcb, gate, grow, ktv, vtv, txb, txf, tk, acc, sts, racc, rsts, mst,
    xs, so, xr, sr, cs, cr, ssem, rsem, lsem, near_sem, far_sem,
):
    ctx = lax.axis_index("ctx")
    zl = lax.axis_index("tp")
    y = ctx // 16
    zh = (ctx // 8) % 2
    x = (ctx // 2) % 4
    c = ctx % 2

    def dev(dy=0, dx=0, flip_c=False, dz=0):
        yy = (y + dy) % NY
        xx = (x + dx) % NX
        zz = (zh * NT + zl + dz + 2 * NT) % (2 * NT)
        cc = 1 - c if flip_c else c
        return (((yy * 2 + zz // NT) * 4 + xx) * 2 + cc, zz % NT)

    def owner(d, p):
        return (((y * 2 + (1 - zh if p else zh)) * 4 + x) * 2 + c, (zl + d) % NT)

    sent = []
    counts = {"s": 0, "r": 0, "l": 0}

    def new(kind):
        counts[kind] += 1
        return counts[kind] - 1

    def send(src, dst, rs, target):
        cp = pltpu.make_async_remote_copy(
            src_ref=src, dst_ref=dst, send_sem=ssem.at[new("s")], recv_sem=rsem.at[rs],
            device_id=target, device_id_type=MESH_ID,
        )
        cp.start()
        sent.append(cp)

    def arrived(ref, rs):
        pltpu.make_async_copy(ref, ref, rsem.at[rs]).wait()

    def fetch(src, dst):
        cp = pltpu.make_async_copy(src, dst, lsem.at[new("l")])
        cp.start()
        return cp

    def signal(sem, target):
        pl.semaphore_signal(sem, inc=1, device_id=target, device_id_type=MESH_ID)

    def cols(h):
        return pl.ds(h * HD, HD)

    barrier = pltpu.get_barrier_semaphore()
    partners = [dev(dx=d) for d in (1, 2, 3)] + [dev(dy=d) for d in (1, 2, 3)]
    partners += [dev(flip_c=True)] + [dev(dz=d) for d in (1, -1, 2, -2)]
    for partner in partners:
        signal(barrier, partner)

    small = [fetch(kt_ref, ktv), fetch(vt_ref, vtv)]
    local = []
    for h in range(NH):
        local.append(fetch(k_ref.at[:, cols(h)], kb.at[h, y, x]))
        local.append(fetch(v_ref.at[:, cols(h)], vb.at[h, y, x]))
        local.append(fetch(q_ref.at[:, cols(h)], qb.at[h, 3]))
    late = [fetch(qc_ref, qcb), fetch(gate_ref, gate)]
    zc = zh * 2 + c
    zo = (1 - zh) * 2 + c
    for cp in small:
        cp.wait()
    txb[zc] = jnp.concatenate(
        [ktv[...].astype(jnp.float32), vtv[...].astype(jnp.float32)], axis=0
    )
    pl.semaphore_wait(barrier, len(partners))

    sib = dev(flip_c=True)
    quarter = 4 - 8 * c

    def table(*shape):
        if not shape:
            return new("r")
        return [table(*shape[1:]) for unused in range(shape[0])]

    r_k1, r_v1 = table(NH, 3), table(NH, 3)
    r_k2, r_v2, r_k3, r_v3 = table(NH, 2), table(NH, 2), table(NH, 2), table(NH, 2)
    r_qs, r_qf, r_qx, r_qy = table(NH), table(NH, 2), table(NH, 2), table(NH)
    r_tf, r_tz, r_ts, r_ty, r_t1, r_t2, r_t3 = (
        table(), table(), table(), table(), table(3), table(3), table()
    )
    r_acc, r_sts, r_x, r_s, r_c = table(NH), table(NH), table(2, NH), table(2), table()

    def first(h):
        for d in (1, 3, 2):
            send(k_ref.at[:, cols(h)], kb.at[h, y, x], r_k1[h][d - 1], dev(dx=d))
            send(v_ref.at[:, cols(h)], vb.at[h, y, x], r_v1[h][d - 1], dev(dy=d))

    def second(h):
        for d in (1, 2, 3):
            arrived(kb.at[h, y, (x - d + NX) % NX], r_k1[h][d - 1])
            arrived(vb.at[h, (y - d + NY) % NY, x], r_v1[h][d - 1])
        for i, d in ((0, 1), (1, 3)):
            send(kb.at[h, y], kb.at[h, y], r_k2[h][i], dev(dy=d))
            send(vb.at[h, :, x], vb.at[h, :, x], r_v2[h][i], dev(dx=d))

    def relay(h):
        for i, d in ((0, 1), (1, 3)):
            yo = (y - d + NY) % NY
            xo = (x - d + NX) % NX
            half = pl.ds(2 * i, 2)
            arrived(kb.at[h, yo], r_k2[h][i])
            send(kb.at[h, yo, half], kb.at[h, yo, half], r_k3[h][i], dev(dy=d))
            arrived(vb.at[h, :, xo], r_v2[h][i])
            send(vb.at[h, half, xo], vb.at[h, half, xo], r_v3[h][i], dev(dx=d))

    def complete(h):
        yo = (y + 2) % NY
        xo = (x + 2) % NX
        for i in range(2):
            half = pl.ds(2 * i, 2)
            arrived(kb.at[h, yo, half], r_k3[h][i])
            arrived(vb.at[h, half, xo], r_v3[h][i])

    def cross(h):
        for i, d in ((0, 4), (1, -4)):
            rows = pl.ds(64 * i, 64)
            send(q_ref.at[rows, cols(h)], qf.at[i, h], r_qf[h][i], dev(dz=d))

    def pass_on(h):
        for i, d in ((0, 4), (1, -4)):
            rows = pl.ds(64 * i, 64)
            arrived(qf.at[i, h], r_qf[h][i])
            send(qf.at[i, h], qb.at[h, 2, rows], r_qx[h][i], dev(dz=d))

    def share(h):
        for i in range(2):
            arrived(qb.at[h, 2, pl.ds(64 * i, 64)], r_qx[h][i])
        send(qb.at[h, 2], qb.at[h, 0], r_qy[h], sib)

    def attend(h):
        arrived(qb.at[h, 1], r_qs[h])
        arrived(qb.at[h, 0], r_qy[h])
        scores = lax.dot_general(
            kb[h].reshape(KEYS, HD), qb[h].reshape(4 * ROWS, HD), (((1,), (1,)), ((), ())),
            preferred_element_type=jnp.float32,
        )
        top = jnp.max(scores, axis=0, keepdims=True)
        weights = jnp.exp2((scores - top) * SCALE2)
        total = jnp.sum(weights, axis=0, keepdims=True)
        product = lax.dot_general(
            vb[h].reshape(KEYS, HD), weights.astype(jnp.bfloat16), (((0,), (0,)), ((), ())),
            preferred_element_type=jnp.float32,
        )
        for b in range(4):
            lanes = slice(b * ROWS, (b + 1) * ROWS)
            acc[h, b] = product[:, lanes]
            sts[h, b] = jnp.concatenate([top[:, lanes], total[:, lanes]], axis=0)
        send(acc.at[h, pl.ds(0, 2)], racc.at[h], r_acc[h], sib)
        send(sts.at[h, pl.ds(0, 2)], rsts.at[h], r_sts[h], sib)

    def merge(h):
        arrived(racc.at[h], r_acc[h])
        arrived(rsts.at[h], r_sts[h])
        for p in (1, 0):
            mine, yours = 3 - p, 1 - p
            one, two = sts[h, mine], rsts[h, yours]
            top = jnp.maximum(one[:1], two[:1])
            f1 = jnp.exp2((one[:1] - top) * SCALE2)
            f2 = jnp.exp2((two[:1] - top) * SCALE2)
            total = one[1:] * f1 + two[1:] * f2
            mixed = acc[h, mine] * (f1 / total) + racc[h, yours] * (f2 / total)
            mixed = mixed.T * grow[:, h * HD : (h + 1) * HD]
            xs[p, h] = mixed.astype(jnp.bfloat16).reshape(NT, CHUNK, HD)
            lane = lax.broadcasted_iota(jnp.int32, (NT, HD), 1)
            packed = jnp.zeros((NT, HD), jnp.float32) if h == 0 else mst[p]
            for k, row in ((h, top), (4 + h, total)):
                moved = jnp.broadcast_to(row, (NT, HD))
                moved = pltpu.roll(moved, 0, 1, stride=CHUNK, stride_axis=0)
                moved = pltpu.roll(moved, (k + 1) * CHUNK % HD, 1)
                packed = jnp.where((lane >> 4) == k, moved, packed)
            if h < NH - 1:
                mst[p] = packed
            else:
                for i in range(NT):
                    so[p, NT - 1 - i] = packed[i : i + 1]
            for d in range(1 - p, NT):
                target = owner(d, p)
                to = (zl + d) % NT
                send(xs.at[p, h, to], xr.at[p, h, zl], r_x[p][h], target)
                if h == NH - 1:
                    send(so.at[p, to], sr.at[p, zl], r_s[p], target)
            if p == 0:
                pltpu.make_async_copy(xs.at[0, h, zl], xr.at[0, h, zl], rsem.at[r_x[0][h]]).start()
                if h == NH - 1:
                    pltpu.make_async_copy(so.at[0, zl], sr.at[0, zl], rsem.at[r_s[0]]).start()

    def text_column():
        arrived(txb.at[zo], r_tz)
        send(txb.at[zo], txb.at[zo], r_ty, sib)
        arrived(txb.at[zh * 2 + 1 - c], r_ts)
        arrived(txb.at[(1 - zh) * 2 + 1 - c], r_ty)
        tiles = [txb[i] for i in range(4)]
        own = jnp.concatenate([jnp.where(c == 0, t[:4], t[4:]) for t in tiles], axis=0)
        tk[c, y, x] = own.astype(jnp.bfloat16)
        for d in (1, 2, 3):
            send(tk.at[c, y, x], tk.at[c, y, x], r_t1[d - 1], dev(dx=d))

    def text_plane():
        for d in (1, 2, 3):
            arrived(tk.at[c, y, (x - d + NX) % NX], r_t1[d - 1])
        for d in (1, 2, 3):
            send(tk.at[c, y], tk.at[c, y], r_t2[d - 1], dev(dy=d))

    def text_core():
        for d in (1, 2, 3):
            arrived(tk.at[c, (y - d + NY) % NY], r_t2[d - 1])
        send(tk.at[c], tk.at[c], r_t3, sib)

    def text_attend():
        arrived(tk.at[1 - c], r_t3)
        j = lax.broadcasted_iota(jnp.int32, (ROWS, TEXT), 1)
        jy, jx, jz, jc, jr = j >> 6, (j >> 4) & 3, (j >> 3) & 1, (j >> 2) & 1, j & 3
        position = ((((jy * 2 + jz) * 4 + jx) * 2 + jc) << 2) + jr
        live = position < text_len[0]
        for h in range(NH):
            lanes = slice(h * HD, (h + 1) * HD)
            text_keys = tk[0].reshape(TEXT, NH * HD)[:, lanes]
            text_values = tk[1].reshape(TEXT, NH * HD)[:, lanes]
            scores = lax.dot_general(
                qcb[:, lanes], text_keys, (((1,), (1,)), ((), ())),
                preferred_element_type=jnp.float32,
            )
            scores = jnp.where(live, scores, -jnp.inf)
            top = jnp.max(scores, axis=1, keepdims=True)
            weights = jnp.exp2((scores - top) * SCALE2)
            total = jnp.sum(weights, axis=1, keepdims=True)
            product = jnp.dot(
                weights.astype(jnp.bfloat16), text_values, preferred_element_type=jnp.float32
            )
            cs[:, :, lanes] = (product / total).astype(jnp.bfloat16).reshape(NT, CHUNK, HD)
        for d in range(1, NT):
            send(cs.at[(zl + d) % NT], cr.at[zl], r_c, owner(d, 0))
        pltpu.make_async_copy(cs.at[zl], cr.at[zl], rsem.at[r_c]).start()

    first(0)
    send(txb.at[zc], txb.at[zc], r_ts, sib)
    for d in (2, -2):
        signal(near_sem, dev(dz=d))
    first(1)
    for h in range(NH):
        send(q_ref.at[:, cols(h)], qb.at[h, 1], r_qs[h], sib)
    pl.semaphore_wait(near_sem, 2)
    for d in (4, -4):
        signal(far_sem, dev(dz=d))
    send(txb.at[zc], txf, r_tf, dev(dz=quarter))
    for h in range(NH):
        cross(h)
    for cp in local:
        cp.wait()
    second(0)
    first(2)
    second(1)
    arrived(txf, r_tf)
    came = ((zh * NT + zl - quarter + 2 * NT) % (2 * NT)) // NT * 2 + c
    send(txf, txb.at[came], r_tz, dev(dz=quarter))
    pass_on(0)
    second(2)
    pass_on(1)
    relay(0)
    pass_on(2)
    pl.semaphore_wait(far_sem, 2)
    text_column()
    share(0)
    relay(1)
    text_plane()
    for cp in late:
        cp.wait()
    here = lax.broadcasted_iota(jnp.int32, gate.shape, 0) == timestep[0]
    grow[...] = jnp.sum(jnp.where(here, gate[...], 0.0), axis=0, keepdims=True)
    complete(0)
    attend(0)
    share(1)
    share(2)
    relay(2)
    merge(0)
    text_core()
    complete(1)
    attend(1)
    text_attend()
    merge(1)
    complete(2)
    attend(2)
    merge(2)

    arrived(cr, r_c)
    for p in range(2):
        for h in range(NH):
            arrived(xr.at[p, h], r_x[p][h])
        arrived(sr.at[p], r_s[p])
    one, two = sr[0].reshape(NT, HD), sr[1].reshape(NT, HD)
    top = jnp.maximum(one, two)
    part1 = pltpu.roll(one, HD // 2, 1) * jnp.exp2((one - top) * SCALE2)
    part2 = pltpu.roll(two, HD // 2, 1) * jnp.exp2((two - top) * SCALE2)
    whole = part1 + part2
    shares = jnp.concatenate(
        [part1 / whole, part2 / whole, jnp.zeros((HD - 2 * NT, HD), jnp.float32)], axis=0
    ).T
    for src in range(NT):
        for h in range(NH):
            rows = slice(h * CHUNK, (h + 1) * CHUNK)
            joined = xr[0, h, src].astype(jnp.float32) * shares[rows, src : src + 1]
            joined += xr[1, h, src].astype(jnp.float32) * shares[rows, NT + src : NT + src + 1]
            joined += cr[src, :, h * HD : (h + 1) * HD].astype(jnp.float32)
            lo = (src * NH + h) * HD
            out_ref[:, lo : lo + HD] = joined.astype(jnp.bfloat16)

    for cp in sent:
        cp.wait_send()
    assert counts["s"] <= SENDS and counts["r"] <= RECVS, counts


def local(q_self, k_self, v_self, q_cross, k_text, v_text, text_len, timestep, gate_table):
    bf16, f32 = jnp.bfloat16, jnp.float32
    smem = pl.BlockSpec(memory_space=pltpu.SMEM)
    vmem = pl.BlockSpec(memory_space=pltpu.VMEM)
    hbm = pl.BlockSpec(memory_space=pltpu.HBM)
    return pl.pallas_call(
        kernel,
        out_shape=jax.ShapeDtypeStruct((CHUNK, NT * NH * HD), bf16),
        in_specs=[smem, smem, hbm, hbm, hbm, hbm, hbm, hbm, hbm],
        out_specs=vmem,
        scratch_shapes=[
            pltpu.VMEM((NH, NY, NX, ROWS, HD), bf16),
            pltpu.VMEM((NH, NY, NX, ROWS, HD), bf16),
            pltpu.VMEM((NH, 4, ROWS, HD), bf16),
            pltpu.VMEM((2, NH, ROWS // 2, HD), bf16),
            pltpu.VMEM((ROWS, NH * HD), bf16),
            pltpu.VMEM(gate_table.shape, f32),
            pltpu.VMEM((1, NH * HD), f32),
            pltpu.VMEM(k_text.shape, bf16),
            pltpu.VMEM(v_text.shape, bf16),
            pltpu.VMEM((4, 8, NH * HD), f32),
            pltpu.VMEM((8, NH * HD), f32),
            pltpu.VMEM((2, NY, NX, 16, NH * HD), bf16),
            pltpu.VMEM((NH, 4, HD, ROWS), f32),
            pltpu.VMEM((NH, 4, 2, ROWS), f32),
            pltpu.VMEM((NH, 2, HD, ROWS), f32),
            pltpu.VMEM((NH, 2, 2, ROWS), f32),
            pltpu.VMEM((2, NT, HD), f32),
            pltpu.VMEM((2, NH, NT, CHUNK, HD), bf16),
            pltpu.VMEM((2, NT, 1, HD), f32),
            pltpu.VMEM((2, NH, NT, CHUNK, HD), bf16),
            pltpu.VMEM((2, NT, 1, HD), f32),
            pltpu.VMEM((NT, CHUNK, NH * HD), bf16),
            pltpu.VMEM((NT, CHUNK, NH * HD), bf16),
            pltpu.SemaphoreType.DMA((SENDS,)),
            pltpu.SemaphoreType.DMA((RECVS,)),
            pltpu.SemaphoreType.DMA((16,)),
            pltpu.SemaphoreType.REGULAR,
            pltpu.SemaphoreType.REGULAR,
        ],
        compiler_params=pltpu.CompilerParams(
            collective_id=0, has_side_effects=True, vmem_limit_bytes=64 * 1024 * 1024
        ),
        name="gated_attention",
    )(text_len, timestep, q_self, k_self, v_self, q_cross, k_text, v_text, gate_table)


def solution(mesh):
    placed = (
        P("ctx", "tp"),
        P("ctx", "tp"),
        P("ctx", "tp"),
        P("ctx", "tp"),
        P("ctx", "tp"),
        P("ctx", "tp"),
        P(),
        P(),
        P(None, "tp"),
    )
    return jax.shard_map(
        local, mesh=mesh, in_specs=placed, out_specs=P(("ctx", "tp"), None), check_vma=False
    )
```

time: 65.6 us -> 61.1 us (0.931)
  Pallas kernels: 62.6 us -> 58.1 us
    pallas_call x1, Pallas kernels: 62.6 us -> 58.1 us  [local(): pl.pallas_call(kernel, out_shape=jax.ShapeDtypeStruct((CHUNK, NT * NH * H...]
where the time goes in v2:
time: 61.1 us; the launch traced here: 61 us
  Pallas kernels  58.1 us (95%)
  local copies, waits for them, and re-layouts  1.54 us (3%)
  between operations  1.3 us (2%)
    pallas_call x1, Pallas kernels, local(): pl.pallas_call(kernel, out_shape=jax.ShapeDtypeStruct((CHUNK, NT * NH * H...  58.1 us
    unnamed x1, local copies, waits for them, and re-layouts  1.54 us

profile of v2, /device:TPU:1, one launch (start us, length us, event | category | flops | bytes accessed | tf_op | source)
XLA Modules:
  0.0 61.0 jit_solution(3172867653057878762)
XLA Ops:
  1.3 58.1 %gated_attention.1 = bf16[16,3072]{1,0:T(8,128)(2,1)} custom-call(s32[1]{0:T(128)S(6)} %copy.11.text_len, s32[1]{0:T(128)S(6)} %copy.12.timestep, bf16[128,384]{1,0:T(8,128)(2,1)} %q_ref.1, bf16[128,384]{1,0:T(8,128)(2,1)} %k_ref.1, bf16[128,384]{1,0:T(8,128)(2,1)} %v_ref.1, bf16[128,384]{1,0:T(8,128)(2,1)} %qc_ref.1, bf16[4,384]{1,0:T(4,128)(2,1)} %kt_ref.1, ...), custom_call_target="tpu_custom_call" | custom-call | tf_op jit(solution)/shard_map/gated_attention/pallas_call | solution.py:346
  59.4 1.5 %copy.13 = bf16[16,3072]{1,0:T(8,128)(2,1)} copy(bf16[16,3072]{1,0:T(8,128)(2,1)} %gated_attention.1) | data formatting | bytes 196608

commit v3 on v2

v3 whole, which is shorter than its diff:
```python
import math

import jax
import jax.numpy as jnp
from jax import lax
from jax.experimental import pallas as pl
from jax.experimental.pallas import tpu as pltpu
from jax.sharding import PartitionSpec as P

HD = 128
ROWS = 128
NH = 3
NX = 4
NY = 4
NT = 8
CHUNK = ROWS // NT
KEYS = NX * NY * ROWS
TEXT = 2 * NX * NY * 16
SCALE2 = HD ** -0.5 * 1.4426950408889634
MESH_ID = pl.DeviceIdType.MESH
SENT = 8679
RECVS = 40


def kernel(
    text_len, timestep, q_ref, k_ref, v_ref, qc_ref, kt_ref, vt_ref, gate_ref, out_ref,
    kb, vb, qb, qf, qcb, gate, grow, ktv, vtv, txb, txf, tk, acc, racc, mst,
    xs, so, xr, sr, cs, cr, tally, ssem, rsem, lsem, near_sem, far_sem,
):
    ctx = lax.axis_index("ctx")
    zl = lax.axis_index("tp")
    y = ctx // 16
    zh = (ctx // 8) % 2
    x = (ctx // 2) % 4
    c = ctx % 2

    def dev(dy=0, dx=0, flip_c=False, dz=0):
        yy = (y + dy) % NY
        xx = (x + dx) % NX
        zz = (zh * NT + zl + dz + 2 * NT) % (2 * NT)
        cc = 1 - c if flip_c else c
        return (((yy * 2 + zz // NT) * 4 + xx) * 2 + cc, zz % NT)

    def owner(d, p):
        return (((y * 2 + (1 - zh if p else zh)) * 4 + x) * 2 + c, (zl + d) % NT)

    counts = {"bytes": 0, "r": 0, "l": 0}

    def new(kind):
        counts[kind] += 1
        return counts[kind] - 1

    def send(src, dst, rs, target):
        pltpu.make_async_remote_copy(
            src_ref=src, dst_ref=dst, send_sem=ssem.at[0], recv_sem=rsem.at[rs],
            device_id=target, device_id_type=MESH_ID,
        ).start()
        counts["bytes"] += math.prod(src.shape) * src.dtype.itemsize

    def arrived(ref, rs):
        pltpu.make_async_copy(ref, ref, rsem.at[rs]).wait()

    def fetch(src, dst, sem):
        cp = pltpu.make_async_copy(src, dst, lsem.at[sem])
        cp.start()
        return cp

    def signal(sem, target):
        pl.semaphore_signal(sem, inc=1, device_id=target, device_id_type=MESH_ID)

    def cols(h):
        return pl.ds(h * HD, HD)

    barrier = pltpu.get_barrier_semaphore()
    partners = [dev(dx=d) for d in (1, 2, 3)] + [dev(dy=d) for d in (1, 2, 3)]
    partners += [dev(flip_c=True)] + [dev(dz=d) for d in (1, -1, 2, -2)]
    for partner in partners:
        signal(barrier, partner)

    for h in range(NH):
        fetch(k_ref.at[:, cols(h)], kb.at[h, 0, 0], 0)
        fetch(v_ref.at[:, cols(h)], vb.at[h, 0, 0], 0)
        fetch(q_ref.at[:, cols(h)], qb.at[h, 3], 0)
    small = [fetch(kt_ref, ktv, 1), fetch(vt_ref, vtv, 2)]
    late = [fetch(qc_ref, qcb, 3), fetch(gate_ref, gate, 4)]
    pl.semaphore_wait(barrier, len(partners))

    sib = dev(flip_c=True)
    quarter = 4 - 8 * c

    def table(*shape):
        if not shape:
            return new("r")
        return [table(*shape[1:]) for unused in range(shape[0])]

    r_1, r_2, r_3 = table(NH), table(NH, 2), table(NH)
    r_qs, r_qf, r_qx, r_qy = table(), table(NH), table(NH), table()
    r_tf, r_tz, r_t, r_t3 = table(), table(), table(), table()
    r_acc, r_x, r_s, r_c = table(NH), table(), table(), table()
    plane = [(dy, dx) for dy in range(NY) for dx in range(NX) if dy + dx]

    def first(h):
        for d in (1, 3, 2):
            send(k_ref.at[:, cols(h)], kb.at[h, 0, 4 - d], r_1[h], dev(dx=d))
            send(v_ref.at[:, cols(h)], vb.at[h, 4 - d, 0], r_1[h], dev(dy=d))

    def halves(i):
        return pl.ds(2 * i, 2), pl.ds(2 - 2 * i, 2)

    def second(h):
        arrived(kb.at[h, pl.ds(0, 2), pl.ds(0, 3)], r_1[h])
        for step in range(2):
            for i, d in ((0, 1), (1, 3)):
                part = halves(i)[step]
                rs = r_3[h] if step else r_2[h][i]
                send(kb.at[h, 0, part], kb.at[h, 4 - d, part], rs, dev(dy=d))
                send(vb.at[h, part, 0], vb.at[h, part, 4 - d], rs, dev(dx=d))

    def relay(h):
        for i, d in ((0, 1), (1, 3)):
            part = halves(i)[0]
            arrived(kb.at[h, 0], r_2[h][i])
            send(kb.at[h, 4 - d, part], kb.at[h, 2, part], r_3[h], dev(dy=d))
            send(vb.at[h, part, 4 - d], vb.at[h, part, 2], r_3[h], dev(dx=d))

    def complete(h):
        arrived(kb.at[h], r_3[h])

    def cross(h):
        for i, d in ((0, 4), (1, -4)):
            rows = pl.ds(64 * i, 64)
            send(q_ref.at[rows, cols(h)], qf.at[i, h], r_qf[h], dev(dz=d))

    def pass_on(h):
        arrived(qb.at[h, 2], r_qf[h])
        for i, d in ((0, 4), (1, -4)):
            send(qf.at[i, h], qb.at[h, 2, pl.ds(64 * i, 64)], r_qx[h], dev(dz=d))

    def share(h):
        arrived(qb.at[h, 2], r_qx[h])
        send(qb.at[h, 2], qb.at[h, 0], r_qy, sib)

    def attend(h):
        scores = lax.dot_general(
            kb[h].reshape(KEYS, HD), qb[h].reshape(4 * ROWS, HD), (((1,), (1,)), ((), ())),
            preferred_element_type=jnp.float32,
        )
        top = jnp.max(scores, axis=0, keepdims=True)
        weights = jnp.exp2((scores - top) * SCALE2)
        total = jnp.sum(weights, axis=0, keepdims=True)
        product = lax.dot_general(
            vb[h].reshape(KEYS, HD), weights.astype(jnp.bfloat16), (((0,), (0,)), ((), ())),
            preferred_element_type=jnp.float32,
        )
        for b in range(4):
            lanes = slice(b * ROWS, (b + 1) * ROWS)
            acc[h, b, :HD] = product[:, lanes]
            acc[h, b, HD : HD + 1] = top[:, lanes]
            acc[h, b, HD + 1 : HD + 2] = total[:, lanes]
        send(acc.at[h, pl.ds(0, 2)], racc.at[h], r_acc[h], sib)

    def merge(h):
        arrived(racc.at[h], r_acc[h])
        for p in (1, 0):
            mine, yours = 3 - p, 1 - p
            one, two = acc[h, mine, HD : HD + 2], racc[h, yours, HD : HD + 2]
            top = jnp.maximum(one[:1], two[:1])
            f1 = jnp.exp2((one[:1] - top) * SCALE2)
            f2 = jnp.exp2((two[:1] - top) * SCALE2)
            total = one[1:] * f1 + two[1:] * f2
            mixed = acc[h, mine, :HD] * (f1 / total) + racc[h, yours, :HD] * (f2 / total)
            mixed = mixed.T * grow[:, h * HD : (h + 1) * HD]
            xs[p, h] = mixed.astype(jnp.bfloat16).reshape(NT, CHUNK, HD)
            lane = lax.broadcasted_iota(jnp.int32, (NT, HD), 1)
            packed = jnp.zeros((NT, HD), jnp.float32) if h == 0 else mst[p]
            for k, row in ((h, top), (4 + h, total)):
                moved = jnp.broadcast_to(row, (NT, HD))
                moved = pltpu.roll(moved, 0, 1, stride=CHUNK, stride_axis=0)
                moved = pltpu.roll(moved, (k + 1) * CHUNK % HD, 1)
                packed = jnp.where((lane >> 4) == k, moved, packed)
            if h < NH - 1:
                mst[p] = packed
            else:
                for i in range(NT):
                    so[p, NT - 1 - i] = packed[i : i + 1]
            for d in range(1 - p, NT):
                target = owner(d, p)
                to = (zl + d) % NT
                send(xs.at[p, h, to], xr.at[p, h, zl], r_x, target)
                if h == NH - 1:
                    send(so.at[p, to], sr.at[p, zl], r_s, target)
            if p == 0:
                pltpu.make_async_copy(xs.at[0, h, zl], xr.at[0, h, zl], rsem.at[r_x]).start()
                if h == NH - 1:
                    pltpu.make_async_copy(so.at[0, zl], sr.at[0, zl], rsem.at[r_s]).start()

    def text_tile():
        arrived(txf, r_tz)
        low, high = txb[0], txb[1]
        own = jnp.concatenate([low[:4], high[:4], low[4:], high[4:]], axis=0)
        tk[c, 0] = own.astype(jnp.bfloat16)
        for dy, dx in plane:
            slot = (-dy % NY) * NX + -dx % NX
            send(tk.at[c, 0], tk.at[c, slot], r_t, dev(dy=dy, dx=dx))

    def text_core():
        arrived(tk.at[c, pl.ds(1, NX * NY - 1)], r_t)
        send(tk.at[c], tk.at[c], r_t3, sib)

    def text_attend():
        arrived(tk.at[1 - c], r_t3)
        j = lax.broadcasted_iota(jnp.int32, (ROWS, TEXT), 1)
        jc, jy, jx = j >> 8, ((j >> 6) + y) & 3, ((j >> 4) + x) & 3
        jz, jr = (j >> 2) & 1, j & 3
        position = ((((jy * 2 + jz) * 4 + jx) * 2 + jc) << 2) + jr
        live = (position < text_len[0]) & ((j & 8) == 0)
        for h in range(NH):
            lanes = slice(h * HD, (h + 1) * HD)
            tiles = tk[:, :, :, lanes].reshape(TEXT, HD)
            scores = lax.dot_general(
                qcb[:, lanes], tiles, (((1,), (1,)), ((), ())), preferred_element_type=jnp.float32
            )
            scores = jnp.where(live, scores, -jnp.inf)
            top = jnp.max(scores, axis=1, keepdims=True)
            weights = jnp.exp2((scores - top) * SCALE2)
            total = jnp.sum(weights, axis=1, keepdims=True)
            moved = pltpu.roll(weights, 8, 1).astype(jnp.bfloat16)
            product = jnp.dot(moved, tiles, preferred_element_type=jnp.float32)
            cs[:, :, lanes] = (product / total).astype(jnp.bfloat16).reshape(NT, CHUNK, HD)
        for d in range(1, NT):
            send(cs.at[(zl + d) % NT], cr.at[zl], r_c, owner(d, 0))
        pltpu.make_async_copy(cs.at[zl], cr.at[zl], rsem.at[r_c]).start()

    for h in range(NH):
        first(h)
    for d in (2, -2):
        signal(near_sem, dev(dz=d))
    for h in range(NH):
        send(q_ref.at[:, cols(h)], qb.at[h, 1], r_qs, sib)
    for cp in small:
        cp.wait()
    txb[zh] = jnp.concatenate(
        [ktv[...].astype(jnp.float32), vtv[...].astype(jnp.float32)], axis=0
    )
    pl.semaphore_wait(near_sem, 2)
    for d in (4, -4):
        signal(far_sem, dev(dz=d))
    send(txb.at[zh], txf, r_tf, dev(dz=quarter))
    for h in range(NH):
        cross(h)
    nine = kb.at[:, 0, pl.ds(0, 3)]
    pltpu.make_async_copy(nine, nine, lsem.at[0]).wait()
    second(0)
    second(1)
    arrived(txf, r_tf)
    source = ((zh * NT + zl - quarter + 2 * NT) % (2 * NT)) // NT
    send(txf, txb.at[source], r_tz, dev(dz=quarter))
    pass_on(0)
    relay(0)
    second(2)
    pass_on(1)
    pass_on(2)
    for cp in late:
        cp.wait()
    here = lax.broadcasted_iota(jnp.int32, gate.shape, 0) == timestep[0]
    grow[...] = jnp.sum(jnp.where(here, gate[...], 0.0), axis=0, keepdims=True)
    text_tile()
    relay(1)
    pl.semaphore_wait(far_sem, 2)
    share(0)
    share(1)
    text_core()
    relay(2)
    share(2)
    text_attend()
    three = kb.at[0, 0, pl.ds(0, 3)]
    arrived(three, r_qs)
    arrived(three, r_qy)
    complete(0)
    attend(0)
    merge(0)
    complete(1)
    attend(1)
    complete(2)
    attend(2)
    merge(1)
    merge(2)

    arrived(cr, r_c)
    arrived(xr, r_x)
    arrived(sr, r_s)
    one, two = sr[0].reshape(NT, HD), sr[1].reshape(NT, HD)
    top = jnp.maximum(one, two)
    part1 = pltpu.roll(one, HD // 2, 1) * jnp.exp2((one - top) * SCALE2)
    part2 = pltpu.roll(two, HD // 2, 1) * jnp.exp2((two - top) * SCALE2)
    whole = part1 + part2
    shares = jnp.concatenate(
        [part1 / whole, part2 / whole, jnp.zeros((HD - 2 * NT, HD), jnp.float32)], axis=0
    ).T
    for src in range(NT):
        for h in range(NH):
            rows = slice(h * CHUNK, (h + 1) * CHUNK)
            joined = xr[0, h, src].astype(jnp.float32) * shares[rows, src : src + 1]
            joined += xr[1, h, src].astype(jnp.float32) * shares[rows, NT + src : NT + src + 1]
            joined += cr[src, :, h * HD : (h + 1) * HD].astype(jnp.float32)
            lo = (src * NH + h) * HD
            out_ref[:, lo : lo + HD] = joined.astype(jnp.bfloat16)

    assert counts["bytes"] == SENT * 512 and counts["r"] <= RECVS, counts
    pltpu.make_async_copy(tally, tally, ssem.at[0]).wait()


def local(q_self, k_self, v_self, q_cross, k_text, v_text, text_len, timestep, gate_table):
    bf16, f32 = jnp.bfloat16, jnp.float32
    smem = pl.BlockSpec(memory_space=pltpu.SMEM)
    vmem = pl.BlockSpec(memory_space=pltpu.VMEM)
    hbm = pl.BlockSpec(memory_space=pltpu.HBM)
    return pl.pallas_call(
        kernel,
        out_shape=jax.ShapeDtypeStruct((CHUNK, NT * NH * HD), bf16),
        in_specs=[smem, smem, hbm, hbm, hbm, hbm, hbm, hbm, hbm],
        out_specs=vmem,
        scratch_shapes=[
            pltpu.VMEM((NH, NY, NX, ROWS, HD), bf16),
            pltpu.VMEM((NH, NY, NX, ROWS, HD), bf16),
            pltpu.VMEM((NH, 4, ROWS, HD), bf16),
            pltpu.VMEM((2, NH, ROWS // 2, HD), bf16),
            pltpu.VMEM((ROWS, NH * HD), bf16),
            pltpu.VMEM(gate_table.shape, f32),
            pltpu.VMEM((1, NH * HD), f32),
            pltpu.VMEM(k_text.shape, bf16),
            pltpu.VMEM(v_text.shape, bf16),
            pltpu.VMEM((2, 8, NH * HD), f32),
            pltpu.VMEM((8, NH * HD), f32),
            pltpu.VMEM((2, NY * NX, 16, NH * HD), bf16),
            pltpu.VMEM((NH, 4, HD + 8, ROWS), f32),
            pltpu.VMEM((NH, 2, HD + 8, ROWS), f32),
            pltpu.VMEM((2, NT, HD), f32),
            pltpu.VMEM((2, NH, NT, CHUNK, HD), bf16),
            pltpu.VMEM((2, NT, 1, HD), f32),
            pltpu.VMEM((2, NH, NT, CHUNK, HD), bf16),
            pltpu.VMEM((2, NT, 1, HD), f32),
            pltpu.VMEM((NT, CHUNK, NH * HD), bf16),
            pltpu.VMEM((NT, CHUNK, NH * HD), bf16),
            pltpu.VMEM((SENT, HD), f32),
            pltpu.SemaphoreType.DMA((1,)),
            pltpu.SemaphoreType.DMA((RECVS,)),
            pltpu.SemaphoreType.DMA((5,)),
            pltpu.SemaphoreType.REGULAR,
            pltpu.SemaphoreType.REGULAR,
        ],
        compiler_params=pltpu.CompilerParams(
            collective_id=0, has_side_effects=True, vmem_limit_bytes=64 * 1024 * 1024
        ),
        name="gated_attention",
    )(text_len, timestep, q_self, k_self, v_self, q_cross, k_text, v_text, gate_table)


def solution(mesh):
    placed = (
        P("ctx", "tp"),
        P("ctx", "tp"),
        P("ctx", "tp"),
        P("ctx", "tp"),
        P("ctx", "tp"),
        P("ctx", "tp"),
        P(),
        P(),
        P(None, "tp"),
    )
    return jax.shard_map(
        local, mesh=mesh, in_specs=placed, out_specs=P(("ctx", "tp"), None), check_vma=False
    )
```

time: 61.1 us -> 56.8 us (0.930)
  Pallas kernels: 58.1 us -> 53.6 us
    pallas_call x1, Pallas kernels: 58.1 us -> 53.6 us  [local(): pl.pallas_call(kernel, out_shape=jax.ShapeDtypeStruct((CHUNK, NT * NH * H...]
where the time goes in v3:
time: 56.8 us; the launch traced here: 56.5 us
  Pallas kernels  53.6 us (94%)
  local copies, waits for them, and re-layouts  1.54 us (3%)
  between operations  1.3 us (2%)
    pallas_call x1, Pallas kernels, local(): pl.pallas_call(kernel, out_shape=jax.ShapeDtypeStruct((CHUNK, NT * NH * H...  53.6 us
    unnamed x1, local copies, waits for them, and re-layouts  1.54 us

profile of v3, /device:TPU:1, one launch (start us, length us, event | category | flops | bytes accessed | tf_op | source)
XLA Modules:
  0.0 56.5 jit_solution(14266394250407371480)
XLA Ops:
  1.3 53.6 %gated_attention.1 = bf16[16,3072]{1,0:T(8,128)(2,1)} custom-call(s32[1]{0:T(128)S(6)} %copy.11.text_len, s32[1]{0:T(128)S(6)} %copy.12.timestep, bf16[128,384]{1,0:T(8,128)(2,1)} %q_ref.1, bf16[128,384]{1,0:T(8,128)(2,1)} %k_ref.1, bf16[128,384]{1,0:T(8,128)(2,1)} %v_ref.1, bf16[128,384]{1,0:T(8,128)(2,1)} %qc_ref.1, bf16[4,384]{1,0:T(4,128)(2,1)} %kt_ref.1, ...), custom_call_target="tpu_custom_call" | custom-call | tf_op jit(solution)/shard_map/gated_attention/pallas_call | solution.py:318
  54.9 1.5 %copy.13 = bf16[16,3072]{1,0:T(8,128)(2,1)} copy(bf16[16,3072]{1,0:T(8,128)(2,1)} %gated_attention.1) | data formatting | bytes 196608

commit v4 on v3

--- a/solution.py
+++ b/solution.py
@@ -257,14 +257,14 @@
     send(txf, txb.at[source], r_tz, dev(dz=quarter))
     pass_on(0)
     relay(0)
+    pass_on(1)
+    text_tile()
     second(2)
-    pass_on(1)
     pass_on(2)
     for cp in late:
         cp.wait()
     here = lax.broadcasted_iota(jnp.int32, gate.shape, 0) == timestep[0]
     grow[...] = jnp.sum(jnp.where(here, gate[...], 0.0), axis=0, keepdims=True)
-    text_tile()
     relay(1)
     pl.semaphore_wait(far_sem, 2)
     share(0)

time: 56.8 us -> 56 us (0.986); the launches traced: 56.5 us -> 55 us
  Pallas kernels: 53.6 us -> 52.1 us
    pallas_call x1, Pallas kernels: 53.6 us -> 52.1 us  [local(): pl.pallas_call(kernel, out_shape=jax.ShapeDtypeStruct((CHUNK, NT * NH * H...]
where the time goes in v4:
time: 56 us; the launch traced here: 55 us
  Pallas kernels  52.1 us (93%)
  local copies, waits for them, and re-layouts  1.54 us (3%)
  between operations  1.3 us (2%)
    pallas_call x1, Pallas kernels, local(): pl.pallas_call(kernel, out_shape=jax.ShapeDtypeStruct((CHUNK, NT * NH * H...  52.1 us
    unnamed x1, local copies, waits for them, and re-layouts  1.54 us

profile of v4, /device:TPU:1, one launch (start us, length us, event | category | flops | bytes accessed | tf_op | source)
XLA Modules:
  0.0 55.0 jit_solution(2752632583379639716)
XLA Ops:
  1.3 52.1 %gated_attention.1 = bf16[16,3072]{1,0:T(8,128)(2,1)} custom-call(s32[1]{0:T(128)S(6)} %copy.11.text_len, s32[1]{0:T(128)S(6)} %copy.12.timestep, bf16[128,384]{1,0:T(8,128)(2,1)} %q_ref.1, bf16[128,384]{1,0:T(8,128)(2,1)} %k_ref.1, bf16[128,384]{1,0:T(8,128)(2,1)} %v_ref.1, bf16[128,384]{1,0:T(8,128)(2,1)} %qc_ref.1, bf16[4,384]{1,0:T(4,128)(2,1)} %kt_ref.1, ...), custom_call_target="tpu_custom_call" | custom-call | tf_op jit(solution)/shard_map/gated_attention/pallas_call | solution.py:318
  53.4 1.5 %copy.13 = bf16[16,3072]{1,0:T(8,128)(2,1)} copy(bf16[16,3072]{1,0:T(8,128)(2,1)} %gated_attention.1) | data formatting | bytes 196608

commit v5 on v4

--- a/solution.py
+++ b/solution.py
@@ -268,8 +268,8 @@
     relay(1)
     pl.semaphore_wait(far_sem, 2)
     share(0)
+    text_core()
     share(1)
-    text_core()
     relay(2)
     share(2)
     text_attend()

time: 56 us -> 56 us (level)
  no operation moved by 1% of the time
where the time goes in v5:
time: 56 us; the launch traced here: 55.1 us
  Pallas kernels  52.2 us (93%)
  local copies, waits for them, and re-layouts  1.54 us (3%)
  between operations  1.3 us (2%)
    pallas_call x1, Pallas kernels, local(): pl.pallas_call(kernel, out_shape=jax.ShapeDtypeStruct((CHUNK, NT * NH * H...  52.2 us
    unnamed x1, local copies, waits for them, and re-layouts  1.54 us

profile of v5, /device:TPU:1, one launch (start us, length us, event | category | flops | bytes accessed | tf_op | source)
XLA Modules:
  0.0 55.1 jit_solution(5280012570299160960)
XLA Ops:
  1.3 52.2 %gated_attention.1 = bf16[16,3072]{1,0:T(8,128)(2,1)} custom-call(s32[1]{0:T(128)S(6)} %copy.11.text_len, s32[1]{0:T(128)S(6)} %copy.12.timestep, bf16[128,384]{1,0:T(8,128)(2,1)} %q_ref.1, bf16[128,384]{1,0:T(8,128)(2,1)} %k_ref.1, bf16[128,384]{1,0:T(8,128)(2,1)} %v_ref.1, bf16[128,384]{1,0:T(8,128)(2,1)} %qc_ref.1, bf16[4,384]{1,0:T(4,128)(2,1)} %kt_ref.1, ...), custom_call_target="tpu_custom_call" | custom-call | tf_op jit(solution)/shard_map/gated_attention/pallas_call | solution.py:318
  53.5 1.5 %copy.13 = bf16[16,3072]{1,0:T(8,128)(2,1)} copy(bf16[16,3072]{1,0:T(8,128)(2,1)} %gated_attention.1) | data formatting | bytes 196608
